TPU v7x, 1024 devices: a whole 8x8x8 slice. The times are simulated.
1024 devices in a mesh: dom: 64 (over y, x), grp: 16 (over z, core).
Axes of the slice: x: 8, y: 8, z: 8, core: 2. Of those that a mesh axis runs over, the one named last changes fastest.
Arguments:
- history: bfloat16 [128, 4, 128, 4096], P('dom', None, 'grp'), may hold values from -6 to 6
- face_patch: int32 [128, 6], replicated, may hold values from -1 to 127, as said below
- refined: int32 [128], replicated, may hold values 0 or 1
- dest_slot: int32 [128], replicated, may hold values from 0 to 127, as said below
- w_in: bfloat16 [640, 512], replicated, may hold values from -0.25 to 0.25
- in_bias: float32 [512], replicated, may hold values from -3 to 3
- w_out: bfloat16 [512, 128], replicated, may hold values from -0.25 to 0.25
Outputs:
- new_states: bfloat16 [128, 2, 128, 4096], P('dom', None, 'grp')
Inputs may be any that keep to these rules, and one draw needn't show every extreme that they name: `dest_slot`: A permutation of the slots. Slot s lies on dom index s // 2; patch p starts at slot p, on index p // 2. No patch moves by more than one index of dom, from one index at most 1 patches go to each neighbouring index, and 1 is reached between some pair of indices. `face_patch`: -1 where the face lies on the window's boundary, else a patch other than p, aligned with p cell for cell on that face; its dom index is within one of p's both before and after rebalancing.
All inputs are finite; a program needn't handle non-finite values.
Results may differ from a plain program's by a relative error of at most 0.0071.
Values may be sent and summed in bfloat16 or wider, within the bound.
A program may use at most 128 MiB of HBM per device.

v0:
```python
import jax
import jax.numpy as jnp
import numpy as np
from jax import lax
from jax.sharding import PartitionSpec as P

SIDE = 16
HIST = 4


OPPOSITE = np.array([1, 0, 3, 2, 5, 4])


def padded(array, sides, width):
    for axis, dim in sides:
        size, length = (lax.axis_size(axis), array.shape[dim])
        up = [(i, (i + 1) % size) for i in range(size - 1)]
        down = [(j, i) for i, j in up]
        last = lax.slice_in_dim(array, length - width, length, axis=dim)
        first = lax.slice_in_dim(array, 0, width, axis=dim)
        before = lax.ppermute(last, axis, up)
        after = lax.ppermute(first, axis, down)
        array = jnp.concatenate([before, array, after], axis=dim)
    return array


def select_table(side_len, stride, offset):
    rows = jnp.arange(side_len)[:, None]
    cols = jnp.arange(side_len * side_len)[None, :]
    return (cols == rows * stride + offset).astype(jnp.bfloat16)


def take_face(grid_rows, table):
    return jnp.einsum("ncxq,kq->ncxk", grid_rows, table, preferred_element_type=jnp.float32).astype(
        jnp.bfloat16
    )


def place_face(face_rows, table):
    return jnp.einsum("ncxk,kq->ncxq", face_rows, table, preferred_element_type=jnp.float32)


def laplace_cells(newest, positions, usable):
    how_many, channels, cell_count = newest.shape
    plane = SIDE * SIDE
    grid_rows = newest.reshape(how_many, channels, SIDE, plane)
    y_low = select_table(SIDE, 1, 0)
    y_high = select_table(SIDE, 1, plane - SIDE)
    z_low = select_table(SIDE, SIDE, 0)
    z_high = select_table(SIDE, SIDE, SIDE - 1)
    layers = jnp.stack(
        [
            grid_rows[:, :, 0, :],
            grid_rows[:, :, -1, :],
            take_face(grid_rows, y_low).reshape(how_many, channels, plane),
            take_face(grid_rows, y_high).reshape(how_many, channels, plane),
            take_face(grid_rows, z_low).reshape(how_many, channels, plane),
            take_face(grid_rows, z_high).reshape(how_many, channels, plane),
        ],
        1,
    )
    layers = layers[:, OPPOSITE]
    beside_all = padded(layers, (("dom", 0),), how_many)
    picked = beside_all[positions, jnp.arange(6)[None, :]]
    picked = jnp.where(usable[:, :, None, None], picked, jnp.zeros_like(picked))
    field = grid_rows.astype(jnp.float32)
    picked_wide = picked.astype(jnp.float32)
    x_plus = jnp.concatenate([field[:, :, 1:, :], picked_wide[:, 1][:, :, None, :]], 2)
    x_minus = jnp.concatenate([picked_wide[:, 0][:, :, None, :], field[:, :, :-1, :]], 2)
    zero_row = jnp.zeros((how_many, channels, SIDE, SIDE), jnp.float32)
    y_plus = jnp.concatenate([field[..., SIDE:], zero_row], 3)
    y_plus = y_plus + place_face(picked[:, 3].reshape(how_many, channels, SIDE, SIDE), y_high)
    y_minus = jnp.concatenate([zero_row, field[..., :-SIDE]], 3)
    y_minus = y_minus + place_face(picked[:, 2].reshape(how_many, channels, SIDE, SIDE), y_low)
    z_index = jnp.arange(plane) % SIDE
    zero_cell = jnp.zeros((how_many, channels, SIDE, 1), jnp.float32)
    z_plus = jnp.concatenate([field[..., 1:], zero_cell], 3)
    z_plus = jnp.where(z_index == SIDE - 1, 0.0, z_plus)
    z_plus = z_plus + place_face(picked[:, 5].reshape(how_many, channels, SIDE, SIDE), z_high)
    z_minus = jnp.concatenate([zero_cell, field[..., :-1]], 3)
    z_minus = jnp.where(z_index == 0, 0.0, z_minus)
    z_minus = z_minus + place_face(picked[:, 4].reshape(how_many, channels, SIDE, SIDE), z_low)
    neighbour_sum = x_plus + x_minus + y_plus + y_minus + z_plus + z_minus
    spread = neighbour_sum - 6.0 * field
    return spread.reshape(how_many, channels, cell_count).astype(jnp.bfloat16)


def local(history, face_patch, refined, dest_slot, w_in, in_bias, w_out):
    per_dev = history.shape[0]
    my_index = lax.axis_index("dom")
    lowest = (my_index - 1) * per_dev
    my_slots = my_index * per_dev + jnp.arange(per_dev, dtype=jnp.int32)
    patch_ids = jnp.arange(dest_slot.shape[0], dtype=jnp.int32)
    inverse = jnp.zeros_like(dest_slot).at[dest_slot].set(patch_ids)

    def advance(inputs):
        how_many = inputs.shape[0]
        cell_count = inputs.shape[3]
        stacked = inputs.reshape(how_many, -1, cell_count)
        preact = (
            jnp.einsum("nkc,kh->nch", stacked, w_in, preferred_element_type=jnp.float32) + in_bias
        )
        hidden = jax.nn.silu(preact).astype(jnp.bfloat16)
        update = jnp.einsum(
            "nch,hk->nkc", hidden, w_out, preferred_element_type=jnp.float32
        ).astype(jnp.bfloat16)
        back = lax.all_to_all(update, "grp", split_axis=1, concat_axis=2, tiled=True)
        return (back, update, inputs[:, : HIST - 1])

    first_nb = face_patch[my_slots]
    first_pos = jnp.clip(first_nb - lowest, 0, 3 * per_dev - 1)
    first_ok = first_nb >= 0
    first_spread = laplace_cells(history[:, 0], first_pos, first_ok)
    first_in = jnp.concatenate([history, first_spread[:, None]], 1)
    first_back, first_cells, first_kept = advance(
        lax.all_to_all(first_in, "grp", split_axis=3, concat_axis=2, tiled=True)
    )
    first_step = 1.0 - 0.5 * refined[my_slots].astype(jnp.float32)
    first_state = (
        history[:, 0].astype(jnp.float32)
        + first_step[:, None, None] * first_back.astype(jnp.float32)
    ).astype(jnp.bfloat16)
    carried = jnp.concatenate([first_state[:, None], history[:, : HIST - 1]], 1)
    owners = inverse[my_slots]
    second_nb = face_patch[owners]
    second_pos = jnp.clip(dest_slot[jnp.maximum(second_nb, 0)] - lowest, 0, 3 * per_dev - 1)
    second_ok = second_nb >= 0
    second_step = 1.0 - 0.5 * refined[owners].astype(jnp.float32)
    sources = inverse[my_slots]
    beside_all = padded(carried.reshape(per_dev, -1), (("dom", 0),), per_dev)
    moved_carried = jnp.take(beside_all, sources - lowest, axis=0).reshape(carried.shape)
    newest = moved_carried[:, 0]
    second_spread = laplace_cells(newest, second_pos, second_ok)
    second_in = jnp.concatenate([moved_carried, second_spread[:, None]], 1)
    second_back, unused_cells, unused_kept = advance(
        lax.all_to_all(second_in, "grp", split_axis=3, concat_axis=2, tiled=True)
    )
    second_state = (
        newest.astype(jnp.float32) + second_step[:, None, None] * second_back.astype(jnp.float32)
    ).astype(jnp.bfloat16)
    return jnp.stack([moved_carried[:, 0], second_state], 1)


def solution(mesh):
    placed = (P("dom", None, "grp", None), P(), P(), P(), P(), P(), P())
    return jax.shard_map(
        local, mesh=mesh, in_specs=placed, out_specs=P("dom", None, "grp", None), check_vma=False
    )
```

profile of v0, /device:TPU:63, one launch (start us, length us, event | category | flops | bytes accessed | tf_op | source)
XLA Modules:
  0.0 287.1 jit_solution(3321924854472272649)
XLA Ops:
  0.0 1.0 slice.95
  1.1 0.3 fusion.14
  1.6 0.3 fusion.15
  2.2 0.3 fusion.16
  2.7 0.3 fusion.17
  3.3 0.7 compare_select_fusion.6
  4.0 1.0 scatter_custom_fusion
  5.0 0.6 gather_fusion
  5.6 0.7 pad_clamp_fusion.2
  6.3 0.5 gather_fusion.3
  6.8 4.3 %collective-permute-start = (bf16[2,6,8,256]{3,2,0,1:T(8,128)(2,1)S(1)}, bf16[2,6,8,256]{3,2,0,1:T(8,128)(2,1)S(1)}, u32[]{:S(2)}, u32[]{:S(2)}) collective-permute-start(bf16[2,6,8,256]{3,2,0,1:T(8,128)(2,1)S(1)} %bitcast.211), channel_id=1, source_target_pairs={{0,16},{16,32},{32,48},{48,64},{64,80},{80,96},{96,112},{112,128},... | collective-permute-start | bytes 147464 | tf_op jit(solution)/shard_map/ppermute | solution.py:21
  11.2 1.9 collective-permute-start.1
  13.1 0.8 copy.129
  13.9 0.6 gather_fusion.2
  14.9 8.7 %copy.135 = bf16[2,4,8,4096]{2,1,0,3:T(4,128)(2,1)} copy(bf16[2,4,8,4096]{3,2,1,0:T(8,128)(2,1)S(1)} %copy-done.3) | data formatting | bytes 1048576 | tf_op args[0]
  23.6 0.6 gather_fusion.4
  24.9 0.2 fusion.9
  25.3 0.2 fusion.7
  25.6 0.2 fusion.10
  25.9 7.3 %copy.136 = bf16[2,1,8,4096]{2,1,0,3:T(2,128)(2,1)} copy(bf16[2,1,8,4096]{3,2,0,1:T(8,128)(2,1)S(1)} %convert_element_type.181) | data formatting | bytes 262144 | tf_op jit(solution)/shard_map/convert_element_type | solution.py:85
  33.2 13.7 %fusion.86 = bf16[4096,2,5,8]{3,2,1,0:T(8,128)(2,1)} fusion(bf16[2,1,8,4096]{2,1,0,3:T(2,128)(2,1)} %copy.136, bf16[2,4,8,4096]{2,1,0,3:T(4,128)(2,1)} %copy.135), kind=kLoop, calls=%fused_computation.178 | loop fusion | flops 1310720 | bytes 1310720
  46.9 17.3 %reshape.347 = bf16[16,2,10240]{2,1,0:T(2,128)(2,1)} reshape(bf16[4096,2,5,8]{3,2,1,0:T(8,128)(2,1)} %fusion.86) | data formatting | bytes 1310720
  64.1 17.6 %all-to-all-start = ((bf16[16,2,10240]{2,1,0:T(2,128)(2,1)}), bf16[16,2,10240]{2,1,0:T(2,128)(2,1)S(1)}, u32[]{:S(2)}, u32[]{:S(2)}) async-start(bf16[16,2,10240]{2,1,0:T(2,128)(2,1)} %reshape.347), calls=%async_computation | async-start | bytes 1310720 | tf_op jit(solution)/shard_map/all_to_all | solution.py:116
  81.8 0.6 gather_fusion.6
  82.5 0.7 gather_fusion.8
  83.1 18.7 %all-to-all-done = bf16[16,2,10240]{2,1,0:T(2,128)(2,1)S(1)} async-done(((bf16[16,2,10240]{2,1,0:T(2,128)(2,1)}), bf16[16,2,10240]{2,1,0:T(2,128)(2,1)S(1)}, u32[]{:S(2)}, u32[]{:S(2)}) %all-to-all-start) | async-done | bytes 655392 | tf_op jit(solution)/shard_map/all_to_all | solution.py:116
  101.8 13.9 %reshape.348 = bf16[4096,2,5,8]{3,2,1,0:T(8,128)(2,1)} reshape(bf16[16,2,10240]{2,1,0:T(2,128)(2,1)S(1)} %all-to-all-done) | data formatting | bytes 1310720
  115.7 14.6 %copy.138 = bf16[2,5,16,8,256]{4,3,2,1,0:T(8,128)(2,1)S(1)} copy(bf16[2,5,16,8,256]{3,1,0,4,2:T(8,128)(2,1)} %bitcast.188) | data formatting | bytes 1310720 | tf_op jit(solution)/shard_map/all_to_all | solution.py:116
  130.3 0.9 fusion.12
  131.2 0.8 copy.140
  132.0 3.4 %all-to-all-start.1 = ((bf16[2,128,256]{2,0,1:T(2,128)(2,1)}), bf16[2,128,256]{2,0,1:T(2,128)(2,1)S(1)}, u32[]{:S(2)}, u32[]{:S(2)}) async-start(bf16[2,128,256]{2,0,1:T(2,128)(2,1)} %copy.140), calls=%async_computation.1 | async-start | bytes 262144 | tf_op jit(solution)/shard_map/all_to_all | solution.py:107
  135.4 0.6 gather_fusion.1
  136.1 7.7 %all-to-all-done.1 = bf16[2,128,256]{2,0,1:T(2,128)(2,1)S(1)} async-done(((bf16[2,128,256]{2,0,1:T(2,128)(2,1)}), bf16[2,128,256]{2,0,1:T(2,128)(2,1)S(1)}, u32[]{:S(2)}, u32[]{:S(2)}) %all-to-all-start.1) | async-done | bytes 131104 | tf_op jit(solution)/shard_map/all_to_all | solution.py:107
  144.1 0.5 copy.167
  144.6 7.0 %collective-permute-start.2 = (bf16[2,131072]{1,0:T(2,128)(2,1)S(1)}, bf16[2,131072]{1,0:T(2,128)(2,1)S(1)}, u32[]{:S(2)}, u32[]{:S(2)}) collective-permute-start(bf16[2,131072]{1,0:T(2,128)(2,1)S(1)} %bitcast.197), channel_id=1, source_target_pairs={{0,16},{16,32},{32,48},{48,64},{64,80},{80,96},{96,112},{112,128},... | collective-permute-start | bytes 1572872 | tf_op jit(solution)/shard_map/ppermute | solution.py:21
  151.6 2.1 collective-permute-start.3
  153.8 9.2 %collective-permute-done.2 = bf16[2,131072]{1,0:T(2,128)(2,1)S(1)} collective-permute-done((bf16[2,131072]{1,0:T(2,128)(2,1)S(1)}, bf16[2,131072]{1,0:T(2,128)(2,1)S(1)}, u32[]{:S(2)}, u32[]{:S(2)}) %collective-permute-start.2) | collective-permute-done | bytes 524320 | tf_op jit(solution)/shard_map/ppermute | solution.py:21
  162.9 7.1 %collective-permute-done.3 = bf16[2,131072]{1,0:T(2,128)(2,1)S(1)} collective-permute-done((bf16[2,131072]{1,0:T(2,128)(2,1)S(1)}, bf16[2,131072]{1,0:T(2,128)(2,1)S(1)}, u32[]{:S(2)}, u32[]{:S(2)}) %collective-permute-start.3) | collective-permute-done | bytes 524320 | tf_op jit(solution)/shard_map/ppermute | solution.py:22
  170.1 1.7 pad_maximum_fusion.1
  171.9 0.9 gather_fusion.10
  172.8 0.9 gather_fusion.11
  173.7 0.5 pad_maximum_fusion.3
  174.2 0.3 copy_select_fusion
  174.7 0.2 convolution_convert_fusion.4
  175.0 0.2 convolution_convert_fusion.3
  175.2 0.2 convolution_convert_fusion.2
  176.0 0.5 gather_fusion.7
  176.6 1.9 collective-permute-start.4
  178.5 3.4 %collective-permute-start.5 = (bf16[2,6,8,256]{3,2,0,1:T(8,128)(2,1)S(1)}, bf16[2,6,8,256]{3,2,0,1:T(8,128)(2,1)S(1)}, u32[]{:S(2)}, u32[]{:S(2)}) collective-permute-start(bf16[2,6,8,256]{3,2,0,1:T(8,128)(2,1)S(1)} %bitcast.215), channel_id=1, source_target_pairs={{16,0},{32,16},{48,32},{64,48},{80,64},{96,80},{112,96},{128,112},... | collective-permute-start | bytes 147464 | tf_op jit(solution)/shard_map/ppermute | solution.py:22
  182.2 4.4 %collective-permute-done.5 = bf16[2,6,8,256]{3,2,0,1:T(8,128)(2,1)S(1)} collective-permute-done((bf16[2,6,8,256]{3,2,0,1:T(8,128)(2,1)S(1)}, bf16[2,6,8,256]{3,2,0,1:T(8,128)(2,1)S(1)}, u32[]{:S(2)}, u32[]{:S(2)}) %collective-permute-start.5) | collective-permute-done | bytes 49184 | tf_op jit(solution)/shard_map/ppermute | solution.py:22
  186.7 0.6 gather_fusion.9
  188.0 0.2 fusion.4
  188.6 0.2 fusion.11
  189.0 13.7 %copy.145 = bf16[2,5,8,4096]{2,1,0,3:T(8,128)(2,1)} copy(bf16[2,5,8,4096]{3,2,0,1:T(8,128)(2,1)S(1)} %pad_maximum_fusion.2) | data formatting | bytes 1310720 | tf_op jit(solution)/shard_map/concatenate | solution.py:134
  202.7 16.5 %reshape.349 = bf16[16,2,10240]{2,1,0:T(2,128)(2,1)S(1)} reshape(bf16[4096,2,5,8]{3,2,1,0:T(8,128)(2,1)} %bitcast.189) | data formatting | bytes 1310720
  219.2 25.0 %all_to_all.48 = bf16[16,2,10240]{2,1,0:T(2,128)(2,1)S(1)} all-to-all(bf16[16,2,10240]{2,1,0:T(2,128)(2,1)S(1)} %reshape.349), channel_id=1, replica_groups=mesh['dom'=64,'grp'=16] {'grp'}, dimensions={0} | all-to-all | bytes 1310720 | tf_op jit(solution)/shard_map/all_to_all | solution.py:136
  244.3 13.9 %reshape.350 = bf16[4096,2,5,8]{3,2,1,0:T(8,128)(2,1)} reshape(bf16[16,2,10240]{2,1,0:T(2,128)(2,1)S(1)} %all_to_all.48) | data formatting | bytes 1310720
  258.1 14.6 %copy.147 = bf16[2,5,16,8,256]{4,3,2,1,0:T(8,128)(2,1)S(1)} copy(bf16[2,5,16,8,256]{3,1,0,4,2:T(8,128)(2,1)} %bitcast.190) | data formatting | bytes 1310720 | tf_op jit(solution)/shard_map/all_to_all | solution.py:136
  272.7 0.9 fusion.13
  273.6 0.8 copy.149
  274.4 3.4 %all-to-all-start.3 = ((bf16[2,128,256]{2,0,1:T(2,128)(2,1)}), bf16[2,128,256]{2,0,1:T(2,128)(2,1)S(1)}, u32[]{:S(2)}, u32[]{:S(2)}) async-start(bf16[2,128,256]{2,0,1:T(2,128)(2,1)} %copy.149), calls=%async_computation.3 | async-start | bytes 262144 | tf_op jit(solution)/shard_map/all_to_all | solution.py:107
  277.8 0.6 gather_fusion.5
  278.4 7.8 %all-to-all-done.3 = bf16[2,128,256]{2,0,1:T(2,128)(2,1)S(1)} async-done(((bf16[2,128,256]{2,0,1:T(2,128)(2,1)}), bf16[2,128,256]{2,0,1:T(2,128)(2,1)S(1)}, u32[]{:S(2)}, u32[]{:S(2)}) %all-to-all-start.3) | async-done | bytes 131104 | tf_op jit(solution)/shard_map/all_to_all | solution.py:107
  286.4 0.7 copy.151
  (108 shorter events, 5.5 us)
Async XLA Ops:
  0.0 130.2 %copy-start = (bf16[640,512]{1,0:T(8,128)(2,1)S(1)}, bf16[640,512]{1,0:T(8,128)(2,1)}, u32[]{:S(2)}) copy-start(bf16[640,512]{1,0:T(8,128)(2,1)} %param.14) | copy-start | bytes 1966084
  0.0 14.8 %copy-start.3 = (bf16[2,4,8,4096]{3,2,1,0:T(8,128)(2,1)S(1)}, bf16[2,4,8,4096]{3,2,1,0:T(8,128)(2,1)}, u32[]{:S(2)}) copy-start(bf16[2,4,8,4096]{3,2,1,0:T(8,128)(2,1)} %param.10) | copy-start | bytes 1572868
  6.8 16.8 %collective-permute-start = (bf16[2,6,8,256]{3,2,0,1:T(8,128)(2,1)S(1)}, bf16[2,6,8,256]{3,2,0,1:T(8,128)(2,1)S(1)}, u32[]{:S(2)}, u32[]{:S(2)}) collective-permute-start(bf16[2,6,8,256]{3,2,0,1:T(8,128)(2,1)S(1)} %bitcast.211), channel_id=1, source_target_pairs={{0,16},{16,32},{32,48},{48,64},{64,80},{80,96},{96,112},{112,128},... | collective-permute-start | bytes 147464 | tf_op jit(solution)/shard_map/ppermute | solution.py:21
  11.2 12.4 %collective-permute-start.1 = (bf16[2,6,8,256]{3,2,0,1:T(8,128)(2,1)S(1)}, bf16[2,6,8,256]{3,2,0,1:T(8,128)(2,1)S(1)}, u32[]{:S(2)}, u32[]{:S(2)}) collective-permute-start(bf16[2,6,8,256]{3,2,0,1:T(8,128)(2,1)S(1)} %bitcast.212), channel_id=1, source_target_pairs={{16,0},{32,16},{48,32},{64,48},{80,64},{96,80},{112,96},{128,112},... | collective-permute-start | bytes 147464 | tf_op jit(solution)/shard_map/ppermute | solution.py:22
  46.9 35.6 %copy-start.1 = (s32[128]{0:T(128)S(1)}, s32[128]{0:T(128)}, u32[]{:S(2)}) copy-start(s32[128]{0:T(128)} %param.13) | copy-start | bytes 1540
  64.1 37.7 %all-to-all-start = ((bf16[16,2,10240]{2,1,0:T(2,128)(2,1)}), bf16[16,2,10240]{2,1,0:T(2,128)(2,1)S(1)}, u32[]{:S(2)}, u32[]{:S(2)}) async-start(bf16[16,2,10240]{2,1,0:T(2,128)(2,1)} %reshape.347), calls=%async_computation | async-start | bytes 1310720 | tf_op jit(solution)/shard_map/all_to_all | solution.py:116
  115.7 14.6 %copy-start.4 = (bf16[512,128]{1,0:T(8,128)(2,1)S(1)}, bf16[512,128]{1,0:T(8,128)(2,1)}, u32[]{:S(2)}) copy-start(bf16[512,128]{1,0:T(8,128)(2,1)} %param.16) | copy-start | bytes 393220
  115.7 14.6 %copy-start.6 = (f32[512]{0:T(512)S(1)}, f32[512]{0:T(512)}, u32[]{:S(2)}) copy-start(f32[512]{0:T(512)} %param.15) | copy-start | bytes 6148
  130.2 5.1 %copy-start.2 = (s32[128]{0:T(128)S(1)}, s32[128]{0:T(128)}, u32[]{:S(2)}) copy-start(s32[128]{0:T(128)} %param.12) | copy-start | bytes 1540
  130.3 13.7 %slice-start = ((bf16[2,4,8,4096]{3,2,1,0:T(8,128)(2,1)}), bf16[2,3,8,4096]{3,2,1,0:T(8,128)(2,1)S(1)}, s32[]{:S(2)}) async-start(bf16[2,4,8,4096]{3,2,1,0:T(8,128)(2,1)} %param.10), calls=%async_computation.4 | async-start | bytes 786432 | tf_op jit(solution)/shard_map/slice | solution.py:123
  132.0 11.9 %all-to-all-start.1 = ((bf16[2,128,256]{2,0,1:T(2,128)(2,1)}), bf16[2,128,256]{2,0,1:T(2,128)(2,1)S(1)}, u32[]{:S(2)}, u32[]{:S(2)}) async-start(bf16[2,128,256]{2,0,1:T(2,128)(2,1)} %copy.140), calls=%async_computation.1 | async-start | bytes 262144 | tf_op jit(solution)/shard_map/all_to_all | solution.py:107
  144.6 18.3 %collective-permute-start.2 = (bf16[2,131072]{1,0:T(2,128)(2,1)S(1)}, bf16[2,131072]{1,0:T(2,128)(2,1)S(1)}, u32[]{:S(2)}, u32[]{:S(2)}) collective-permute-start(bf16[2,131072]{1,0:T(2,128)(2,1)S(1)} %bitcast.197), channel_id=1, source_target_pairs={{0,16},{16,32},{32,48},{48,64},{64,80},{80,96},{96,112},{112,128},... | collective-permute-start | bytes 1572872 | tf_op jit(solution)/shard_map/ppermute | solution.py:21
  151.6 18.5 %collective-permute-start.3 = (bf16[2,131072]{1,0:T(2,128)(2,1)S(1)}, bf16[2,131072]{1,0:T(2,128)(2,1)S(1)}, u32[]{:S(2)}, u32[]{:S(2)}) collective-permute-start(bf16[2,131072]{1,0:T(2,128)(2,1)S(1)} %bitcast.198), channel_id=1, source_target_pairs={{16,0},{32,16},{48,32},{64,48},{80,64},{96,80},{112,96},{128,112},... | collective-permute-start | bytes 1572872 | tf_op jit(solution)/shard_map/ppermute | solution.py:22
  176.6 5.6 %collective-permute-start.4 = (bf16[2,6,8,256]{3,2,0,1:T(8,128)(2,1)S(1)}, bf16[2,6,8,256]{3,2,0,1:T(8,128)(2,1)S(1)}, u32[]{:S(2)}, u32[]{:S(2)}) collective-permute-start(bf16[2,6,8,256]{3,2,0,1:T(8,128)(2,1)S(1)} %bitcast.214), channel_id=1, source_target_pairs={{0,16},{16,32},{32,48},{48,64},{64,80},{80,96},{96,112},{112,128},... | collective-permute-start | bytes 147464 | tf_op jit(solution)/shard_map/ppermute | solution.py:21
  178.5 8.2 %collective-permute-start.5 = (bf16[2,6,8,256]{3,2,0,1:T(8,128)(2,1)S(1)}, bf16[2,6,8,256]{3,2,0,1:T(8,128)(2,1)S(1)}, u32[]{:S(2)}, u32[]{:S(2)}) collective-permute-start(bf16[2,6,8,256]{3,2,0,1:T(8,128)(2,1)S(1)} %bitcast.215), channel_id=1, source_target_pairs={{16,0},{32,16},{48,32},{64,48},{80,64},{96,80},{112,96},{128,112},... | collective-permute-start | bytes 147464 | tf_op jit(solution)/shard_map/ppermute | solution.py:22
  258.1 14.6 %copy-start.5 = (bf16[512,128]{1,0:T(8,128)(2,1)S(1)}, bf16[512,128]{1,0:T(8,128)(2,1)}, u32[]{:S(2)}) copy-start(bf16[512,128]{1,0:T(8,128)(2,1)} %param.16) | copy-start | bytes 393220
  274.4 11.9 %all-to-all-start.3 = ((bf16[2,128,256]{2,0,1:T(2,128)(2,1)}), bf16[2,128,256]{2,0,1:T(2,128)(2,1)S(1)}, u32[]{:S(2)}, u32[]{:S(2)}) async-start(bf16[2,128,256]{2,0,1:T(2,128)(2,1)} %copy.149), calls=%async_computation.3 | async-start | bytes 262144 | tf_op jit(solution)/shard_map/all_to_all | solution.py:107
where the time goes:
time: 289 us; the launch traced here: 287 us
  local copies, waits for them, and re-layouts  138 us (48%)
  waiting for transfers between devices  54.9 us (19%)
  starting transfers between devices  45.1 us (16%)
  blocking collectives  25 us (9%)
  other arithmetic  18.3 us (6%)
  matrix products  5.47 us (2%)
    unnamed x31, local copies, waits for them, and re-layouts  71.5 us
    all_to_all x1, blocking collectives, local(): lax.all_to_all(second_in, 'grp', split_axis=3, concat_axis=2, tiled=True)  25 us
    all_to_all x1, waiting for transfers between devices, local(): lax.all_to_all(first_in, 'grp', split_axis=3, concat_axis=2, tiled=True)  18.7 us
    all_to_all x1, starting transfers between devices, local(): lax.all_to_all(first_in, 'grp', split_axis=3, concat_axis=2, tiled=True)  17.6 us
    all_to_all x2, waiting for transfers between devices, advance(): lax.all_to_all(update, 'grp', split_axis=1, concat_axis=2, tiled=True)  15.5 us
    all_to_all x1, local copies, waits for them, and re-layouts, local(): lax.all_to_all(first_in, 'grp', split_axis=3, concat_axis=2, tiled=True)  14.6 us
    all_to_all x1, local copies, waits for them, and re-layouts, local(): lax.all_to_all(second_in, 'grp', split_axis=3, concat_axis=2, tiled=True)  14.6 us
    unnamed x3, other arithmetic  14.2 us
  transfers between devices with their start and end apart: 9, of which 6 were waited for; matrix products, arithmetic and copies ran while one was open for 5% of the time, Pallas kernels for 0%

commit v1 on v0

v1 whole, which is shorter than its diff:
```python
import functools

import jax
import jax.numpy as jnp
from jax import lax
from jax.experimental import pallas as pl
from jax.experimental.pallas import tpu as pltpu
from jax.sharding import PartitionSpec as P

MESH = pl.DeviceIdType.MESH
F32, BF16 = jnp.float32, jnp.bfloat16


def surrogate(sizes, dest, face, refined, hist, w_in, w_out, bias, out, own, stage, moved, mine, cells, state1, state2,
              xm1, xp1, xm2, xp2, edge1, edge2, w_raw, wo_raw, wt, wot, bcol, feed, base, adj, pick, place,
              load_sem, mig_send, mig_recv, go_send, go_recv, back_send, back_recv, halo_send, halo_recv):
    doms, grps, side, hist_len, ch, hid = sizes
    plane = side * side
    block = ch // grps
    d, g = lax.axis_index("dom"), lax.axis_index("grp")
    left, right = lax.rem(d + doms - 1, doms), lax.rem(d + 1, doms)
    up, down = lax.rem(g + 1, grps), lax.rem(g + grps - 1, grps)
    my_plane = down

    def wait_for(ref, sem):
        pltpu.make_async_copy(ref, ref, sem).wait()

    loads = [pltpu.make_async_copy(hist.at[:, k], own.at[k], load_sem.at[k]) for k in range(hist_len)]
    loads.append(pltpu.make_async_copy(w_in, w_raw, load_sem.at[hist_len]))
    loads.append(pltpu.make_async_copy(w_out, wo_raw, load_sem.at[hist_len + 1]))
    for load in loads:
        load.start()

    barrier = pltpu.get_barrier_semaphore()

    def greet(i, carry):
        pl.semaphore_signal(barrier, inc=1, device_id=(d, lax.rem(g + i, grps)), device_id_type=MESH)
        return carry

    lax.fori_loop(1, grps, greet, 0)
    for beside in (left, right):
        pl.semaphore_signal(barrier, inc=1, device_id=(beside, g), device_id_type=MESH)

    @pl.when(g < 2)
    def _():
        for beside in (left, right):
            pl.semaphore_signal(barrier, inc=1, device_id=(beside, 1 - g), device_id_type=MESH)

    patches = 2 * doms
    cands = [lax.rem(2 * d + patches - 2 + i, patches) for i in range(6)]
    goals = [dest[c] for c in cands]
    go_left = jnp.where(goals[3] // 2 == d - 1, 1, 0)
    go_right = jnp.where(goals[3] // 2 == d + 1, 1, 0)
    origin, beside_slot, step_size = [], [], []
    for j in range(2):
        place_of = jnp.int32(0)
        owner = jnp.int32(0)
        for i in range(6):
            hit = goals[i] == 2 * d + j
            place_of = jnp.where(hit, i, place_of)
            owner = jnp.where(hit, cands[i], owner)
        origin.append(place_of)
        row = []
        for f in range(6):
            q = face[f, owner]
            pos = jnp.clip(dest[jnp.maximum(q, 0)] - 2 * (d - 1), 0, 5)
            row.append(jnp.where(q >= 0, pos, 6))
        beside_slot.append(row)
        step_size.append(1.0 - 0.5 * refined[owner].astype(F32))

    for buf in (xm1, xp1, xm2, xp2):
        buf[6] = jnp.zeros(buf.shape[1:], BF16)

    for k in range(hist_len):
        loads[k].wait()
    pl.semaphore_wait(barrier, jnp.where(g < 2, grps + 3, grps + 1))

    moves = []
    for k in range(hist_len):
        for side_of, (which, target) in enumerate(((go_right, right), (go_left, left))):
            stage[k, side_of] = jnp.where(which == 1, own[k, 1], own[k, 0])
            move = pltpu.make_async_remote_copy(
                src_ref=stage.at[k, side_of], dst_ref=moved.at[k, side_of], send_sem=mig_send.at[k, side_of],
                recv_sem=mig_recv.at[k, side_of], device_id=(target, g), device_id_type=MESH)
            move.start()
            moves.append(move)

    def lanes_of(device):
        return pl.ds(pl.multiple_of(lax.rem(device + grps - 1, grps) * plane, plane), plane)

    for k in range(hist_len):
        moves[2 * k].wait_recv()
        moves[2 * k + 1].wait_recv()
        for j in range(2):
            at = origin[j]
            stays = jnp.where(at == 2, own[k, 0], own[k, 1])
            comes = jnp.where(at < 2, moved[k, 0], moved[k, 1])
            mine[k, j] = jnp.where((at == 2) | (at == 3), stays, comes)

        def send(i, carry, k=k):
            peer = lax.rem(g + i, grps)
            pltpu.make_async_remote_copy(
                src_ref=mine.at[k, :, :, lanes_of(peer)], dst_ref=cells.at[k, :, g], send_sem=go_send.at[k],
                recv_sem=go_recv.at[k], device_id=(d, peer), device_id_type=MESH).start()
            return carry

        lax.fori_loop(1, grps, send, 0)
        pltpu.make_async_copy(mine.at[k, :, :, lanes_of(g)], cells.at[k, :, g], go_recv.at[k]).start()

    r = lax.broadcasted_iota(jnp.int32, (plane, plane), 0)
    c = lax.broadcasted_iota(jnp.int32, (plane, plane), 1)
    ry, rz, cy, cz = r // side, r % side, c // side, c % side
    beside_cell = ((ry == cy) & (jnp.abs(rz - cz) == 1)) | ((rz == cz) & (jnp.abs(ry - cy) == 1))
    adj[...] = jnp.where(r == c, -6.0, jnp.where(beside_cell, 1.0, 0.0)).astype(BF16)
    width = 8 * side

    def layer_cell(layer, k):
        along_y = jnp.where(layer == 0, k, plane - side + k)
        along_z = jnp.where(layer == 2, k * side, k * side + side - 1)
        return jnp.where(layer < 2, along_y, along_z)

    r = lax.broadcasted_iota(jnp.int32, (plane, width), 0)
    c = lax.broadcasted_iota(jnp.int32, (plane, width), 1)
    for j in range(2):
        hit = (r == layer_cell((c // side) % 4, c % side)) & (c // (4 * side) == j)
        pick[j] = jnp.where(hit, 1.0, 0.0).astype(BF16)
    r = lax.broadcasted_iota(jnp.int32, (width, plane), 0)
    c = lax.broadcasted_iota(jnp.int32, (width, plane), 1)
    layer = (r // side) % 4
    opposite = jnp.where(layer % 2 == 0, layer + 1, layer - 1)
    place[...] = jnp.where(c == layer_cell(opposite, r % side), 1.0, 0.0).astype(BF16)
    bcol[...] = jnp.broadcast_to(bias[...], (bcol.shape[1], hid)).T
    loads[hist_len].wait()
    loads[hist_len + 1].wait()
    for k in range(hist_len + 1):
        wt[:, k * ch:(k + 1) * ch] = w_raw[k * ch:(k + 1) * ch, :].astype(F32).T.astype(BF16)
    wot[...] = wo_raw[...].astype(F32).T.astype(BF16)

    lane = lax.broadcasted_iota(jnp.int32, (ch, width), 1)
    lane_layer, lane_patch = (lane // side) % 4, lane // (4 * side)

    def wide(ref_value):
        return ref_value.astype(F32).reshape(ch, plane)

    def start_halo(t, state, xm, xp, edge):
        rows = [wide(state[j]).astype(BF16) for j in range(2)]
        edges = sum(jnp.dot(rows[j], pick[j], preferred_element_type=F32) for j in range(2))
        edge[1] = edges.astype(BF16)
        plans = [(state, xm.at[pl.ds(2, 2)], (d, up)), (state, xp.at[pl.ds(2, 2)], (d, down)),
                 (edge.at[1], edge.at[0], (right, g)), (edge.at[1], edge.at[2], (left, g))]
        copies = [pltpu.make_async_remote_copy(
            src_ref=src, dst_ref=dst, send_sem=halo_send.at[t, i], recv_sem=halo_recv.at[t, i], device_id=to,
            device_id_type=MESH) for i, (src, dst, to) in enumerate(plans)]

        def over_the_rim(buf):
            return [pltpu.make_async_remote_copy(
                src_ref=state, dst_ref=buf.at[pl.ds(at, 2)], send_sem=halo_send.at[t, 4 + i],
                recv_sem=halo_recv.at[t, 4 + i], device_id=(to, 1 - g), device_id_type=MESH)
                for i, (at, to) in enumerate(((0, right), (4, left)))]

        @pl.when(g == 0)
        def _():
            for copy in over_the_rim(xm):
                copy.start()

        @pl.when(g == 1)
        def _():
            for copy in over_the_rim(xp):
                copy.start()

        for copy in copies:
            copy.start()

        def finish():
            for copy in copies:
                copy.wait()

            @pl.when(g == 0)
            def _():
                for copy in over_the_rim(xp):
                    copy.wait()

            @pl.when(g == 1)
            def _():
                for copy in over_the_rim(xm):
                    copy.wait()

        return finish

    def laplace(state, xm, xp, edge, j):
        near = jnp.dot(wide(state[j]).astype(BF16), adj[...], preferred_element_type=F32)
        slots = beside_slot[j]
        wanted = jnp.where(lane_layer == 0, slots[3], jnp.where(lane_layer == 1, slots[2], jnp.where(
            lane_layer == 2, slots[5], slots[4])))
        faces = jnp.zeros((ch, width), F32)
        for i in range(3):
            faces = jnp.where(wanted == 2 * i + lane_patch, edge[i].astype(F32), faces)
        near = near + jnp.dot(faces.astype(BF16), place[...], preferred_element_type=F32)
        before = xm[jnp.where(my_plane == 0, slots[0], 2 + j)]
        after = xp[jnp.where(my_plane == grps - 1, slots[1], 2 + j)]
        return (near + wide(before) + wide(after)).astype(BF16)

    def beside_bias(value):
        return value + jnp.concatenate([bcol[...]] * (plane // bcol.shape[1]), 1)

    def next_state(pre, start, j):
        hidden = (pre / (1.0 + jnp.exp(-pre))).astype(BF16)
        update = jnp.dot(wot[...], hidden, preferred_element_type=F32).astype(BF16)
        fresh = start + step_size[j] * update.astype(F32)
        return fresh.reshape(grps, block, plane).astype(BF16)

    def send_back(t, state):
        def send(i, carry):
            peer = lax.rem(g + i, grps)
            pltpu.make_async_remote_copy(
                src_ref=state.at[:, peer], dst_ref=out.at[:, t, :, lanes_of(g)], send_sem=back_send.at[t],
                recv_sem=back_recv.at[t], device_id=(d, peer), device_id_type=MESH).start()
            return carry

        lax.fori_loop(1, grps, send, 0)
        pltpu.make_async_copy(state.at[:, g], out.at[:, t, :, lanes_of(g)], back_recv.at[t]).start()

    newest = cells.at[0]
    wait_for(newest, go_recv.at[0])
    finish1 = start_halo(0, newest, xm1, xp1, edge1)
    for k in range(hist_len):
        if k > 0:
            wait_for(cells.at[k], go_recv.at[k])
        for j in range(2):
            feed[k * ch:(k + 1) * ch, j * plane:(j + 1) * plane] = wide(cells[k, j]).astype(BF16)
    finish1()
    for j in range(2):
        cols = slice(j * plane, (j + 1) * plane)
        feed[hist_len * ch:, cols] = laplace(newest, xm1, xp1, edge1, j)
        pre = beside_bias(jnp.dot(wt[...], feed[:, cols], preferred_element_type=F32))
        state1[j] = next_state(pre, wide(newest[j]), j)

    finish2 = start_halo(1, state1, xm2, xp2, edge2)
    send_back(0, state1)
    for j in range(2):
        cols = slice(j * plane, (j + 1) * plane)
        kept = jnp.dot(wt[:, ch:hist_len * ch], feed[:(hist_len - 1) * ch, cols], preferred_element_type=F32)
        fresh = jnp.dot(wt[:, :ch], wide(state1[j]).astype(BF16), preferred_element_type=F32)
        base[:, cols] = beside_bias(kept + fresh)
    finish2()
    for j in range(2):
        cols = slice(j * plane, (j + 1) * plane)
        spread = laplace(state1, xm2, xp2, edge2, j)
        pre = base[:, cols] + jnp.dot(wt[:, hist_len * ch:], spread, preferred_element_type=F32)
        state2[j] = next_state(pre, wide(state1[j]), j)
    send_back(1, state2)

    for move in moves:
        move.wait_send()
    for k in range(hist_len):
        wait_for(cells.at[k, :, pl.ds(0, grps - 1)], go_send.at[k])
    for t in range(2):
        wait_for(state1.at[:, pl.ds(0, grps - 1)], back_send.at[t])
        wait_for(out.at[:, t], back_recv.at[t])


def solution(mesh):
    doms, grps = mesh.shape["dom"], mesh.shape["grp"]

    def local(history, face_patch, refined, dest_slot, w_in, in_bias, w_out):
        per_dev, hist_len, block, cell_count = history.shape
        hid, ch = w_out.shape
        side = round(cell_count ** (1 / 3))
        plane = side * side
        width = 8 * side
        sizes = (doms, grps, side, hist_len, ch, hid)
        smem = pl.BlockSpec(memory_space=pltpu.SMEM)
        anywhere = pl.BlockSpec(memory_space=pl.ANY)
        vmem, dma = pltpu.VMEM, pltpu.SemaphoreType.DMA
        column = min(128, plane)
        return pl.pallas_call(
            functools.partial(surrogate, sizes),
            out_shape=jax.ShapeDtypeStruct((per_dev, 2, block, cell_count), BF16),
            in_specs=[smem, smem, smem, anywhere, anywhere, anywhere, pl.BlockSpec(memory_space=pltpu.VMEM)],
            out_specs=anywhere,
            scratch_shapes=[
                vmem((hist_len, per_dev, block, cell_count), BF16),
                vmem((hist_len, 2, block, cell_count), BF16),
                vmem((hist_len, 2, block, cell_count), BF16),
                vmem((hist_len, per_dev, block, cell_count), BF16),
                vmem((hist_len, per_dev, grps, block, plane), BF16),
                vmem((per_dev, grps, block, plane), BF16),
                vmem((per_dev, grps, block, plane), BF16),
                *[vmem((7, grps, block, plane), BF16) for _ in range(4)],
                *[vmem((3, ch, width), BF16) for _ in range(2)],
                vmem(w_in.shape, BF16),
                vmem(w_out.shape, BF16),
                vmem((hid, w_in.shape[0]), BF16),
                vmem((ch, hid), BF16),
                vmem((hid, column), F32),
                vmem((w_in.shape[0], per_dev * plane), BF16),
                vmem((hid, per_dev * plane), F32),
                vmem((plane, plane), BF16),
                vmem((2, plane, width), BF16),
                vmem((width, plane), BF16),
                dma((hist_len + 2,)),
                dma((hist_len, 2)),
                dma((hist_len, 2)),
                dma((hist_len,)),
                dma((hist_len,)),
                dma((2,)),
                dma((2,)),
                dma((2, 6)),
                dma((2, 6)),
            ],
            compiler_params=pltpu.CompilerParams(
                collective_id=0, has_side_effects=True, vmem_limit_bytes=60 * 2**20),
            name="surrogate",
        )(dest_slot, face_patch.T, refined, history, w_in, w_out, in_bias.reshape(1, hid))

    placed = (P("dom", None, "grp", None), P(), P(), P(), P(), P(), P())
    return jax.shard_map(
        local, mesh=mesh, in_specs=placed, out_specs=P("dom", None, "grp", None), check_vma=False
    )
```

time: 289 us -> 58.3 us (0.20)
  the two profiles are of different devices: /device:TPU:63 before, /device:TPU:1 now
where the time goes in v1:
time: 58.3 us; the launch traced here: 58.1 us
  Pallas kernels  56.4 us (97%)
  local copies, waits for them, and re-layouts  1.67 us (3%)
    pallas_call x1, Pallas kernels, local(): pl.pallas_call(functools.partial(surrogate, sizes), out_shape=jax.ShapeDt...  56.4 us
    unnamed x1, local copies, waits for them, and re-layouts  1.67 us

profile of v1, /device:TPU:1, one launch (start us, length us, event | category | flops | bytes accessed | tf_op | source)
XLA Modules:
  0.0 58.1 jit_solution(15037067189316595464)
XLA Ops:
  0.0 56.4 %surrogate.1 = bf16[2,2,8,4096]{3,2,1,0:T(8,128)(2,1)} custom-call(s32[128]{0:T(128)} %dest.1, s32[6,128]{1,0:T(8,128)} %bitcast.2, s32[128]{0:T(128)} %refined.1, bf16[2,4,8,4096]{3,2,1,0:T(8,128)(2,1)} %hist.1, bf16[640,512]{1,0:T(8,128)(2,1)} %w_in.1, bf16[512,128]{1,0:T(8,128)(2,1)} %w_out.1, f32[1,512]{1,0:T(1,128)} %bitcast.3), custom_call_target="tpu_custom_call" | custom-call | tf_op jit(solution)/shard_map/surrogate/pallas_call | solution.py:276
  56.4 1.7 %copy.9 = bf16[2,2,8,4096]{3,2,1,0:T(8,128)(2,1)} copy(bf16[2,2,8,4096]{3,2,1,0:T(8,128)(2,1)} %surrogate.1) | data formatting | bytes 524288

commit v2 on v1

v2 whole, which is shorter than its diff:
```python
import functools

import jax
import jax.numpy as jnp
from jax import lax
from jax.experimental import pallas as pl
from jax.experimental.pallas import tpu as pltpu
from jax.sharding import PartitionSpec as P

MESH = pl.DeviceIdType.MESH
F32, BF16 = jnp.float32, jnp.bfloat16


def surrogate(sizes, dest, face, refined, hist, w_in, w_out, bias, out, own, stage, moved, mine, cells, last, stage_last,
              moved_last, state1, state2, xm1, xp1, xm2, xp2, edge1, edge2, w_raw, wo_raw, wt, wot, bcol, base1, base2,
              adj, pick, place, load_sem, mig_send, mig_recv, go_send, go_recv, back_send, back_recv, halo_send,
              halo_recv):
    doms, grps, side, hist_len, ch, hid = sizes
    plane = side * side
    block = ch // grps
    oldest = hist_len - 1
    d, g = lax.axis_index("dom"), lax.axis_index("grp")
    left, right = d - 1, d + 1
    has_left, has_right = d > 0, d < doms - 1
    up, down = lax.rem(g + 1, grps), lax.rem(g + grps - 1, grps)
    my_plane = down

    def wait_for(ref, sem):
        pltpu.make_async_copy(ref, ref, sem).wait()

    def remote(src, dst, send_sem, recv_sem, to):
        return pltpu.make_async_remote_copy(
            src_ref=src, dst_ref=dst, send_sem=send_sem, recv_sem=recv_sem, device_id=to, device_id_type=MESH)

    loads = [pltpu.make_async_copy(hist.at[:, k], own.at[k], load_sem.at[k]) for k in range(hist_len)]
    loads.append(pltpu.make_async_copy(w_in, w_raw, load_sem.at[hist_len]))
    loads.append(pltpu.make_async_copy(w_out, wo_raw, load_sem.at[hist_len + 1]))

    barrier = pltpu.get_barrier_semaphore()

    def greet(i, carry):
        pl.semaphore_signal(barrier, inc=1, device_id=(d, lax.rem(g + i, grps)), device_id_type=MESH)
        return carry

    lax.fori_loop(1, grps, greet, 0)
    for there, beside in ((has_left, left), (has_right, right)):
        @pl.when(there)
        def _(beside=beside):
            pl.semaphore_signal(barrier, inc=1, device_id=(beside, g), device_id_type=MESH)

            @pl.when(g < 2)
            def _():
                pl.semaphore_signal(barrier, inc=1, device_id=(beside, 1 - g), device_id_type=MESH)

    for load in loads:
        load.start()

    patches = 2 * doms
    cands = [lax.rem(2 * d + patches - 2 + i, patches) for i in range(6)]
    goals = [dest[c] for c in cands]
    go_left = jnp.where(goals[3] // 2 == d - 1, 1, 0)
    go_right = jnp.where(goals[3] // 2 == d + 1, 1, 0)
    origin, beside_slot, step_size = [], [], []
    for j in range(2):
        place_of = jnp.int32(0)
        owner = jnp.int32(0)
        for i in range(6):
            hit = goals[i] == 2 * d + j
            place_of = jnp.where(hit, i, place_of)
            owner = jnp.where(hit, cands[i], owner)
        origin.append(place_of)
        row = []
        for f in range(6):
            q = face[f, owner]
            pos = jnp.clip(dest[jnp.maximum(q, 0)] - 2 * (d - 1), 0, 5)
            row.append(jnp.where(q >= 0, pos, 6))
        beside_slot.append(row)
        step_size.append(1.0 - 0.5 * refined[owner].astype(F32))

    def placed(j, mine_of, from_left, from_right):
        at = origin[j]
        stays = jnp.where(at == 2, mine_of(0), mine_of(1))
        comes = jnp.where(at < 2, from_left, from_right)
        return jnp.where((at == 2) | (at == 3), stays, comes)

    for buf in (xm1, xp1, xm2, xp2):
        buf[6] = jnp.zeros(buf.shape[1:], BF16)
    for k in range(hist_len):
        loads[k].wait()
    beside_count = jnp.where(has_left, 1, 0) + jnp.where(has_right, 1, 0)
    pl.semaphore_wait(barrier, grps - 1 + beside_count * jnp.where(g < 2, 2, 1))

    def sent(src, dst, k):
        return [(has_right, remote(src.at[0], dst.at[0], mig_send.at[k, 0], mig_recv.at[k, 0], (right, g))),
                (has_left, remote(src.at[1], dst.at[1], mig_send.at[k, 1], mig_recv.at[k, 1], (left, g)))]

    def move(k):
        for to, which in enumerate((go_right, go_left)):
            stage[k, to] = jnp.where(which == 1, own[k, 1], own[k, 0])
        start_moves(stage.at[k], moved.at[k], k)

    def start_moves(src, dst, k):
        for there, copy in sent(src, dst, k):
            pl.when(there)(copy.start)

    def arrived(src, dst, k):
        (_, from_left), (_, from_right) = sent(src, dst, k)
        pl.when(has_left)(from_left.wait_recv)
        pl.when(has_right)(from_right.wait_recv)

    def lanes_of(device):
        return pl.ds(pl.multiple_of(lax.rem(device + grps - 1, grps) * plane, plane), plane)

    def far_first(i):
        half = lax.div(i, 2)
        return lax.rem(g + grps // 2 + jnp.where(lax.rem(i, 2) == 0, half, -half), grps)

    def spread_planes(src, dst, k):
        def send(i, carry):
            peer = far_first(i)
            remote(src.at[:, :, lanes_of(peer)], dst.at[:, g], go_send.at[k], go_recv.at[k], (d, peer)).start()
            return carry

        lax.fori_loop(1, grps, send, 0)
        pltpu.make_async_copy(src.at[:, :, lanes_of(g)], dst.at[:, g], go_recv.at[k]).start()

    def settle(k):
        arrived(stage.at[k], moved.at[k], k)
        for j in range(2):
            mine[k, j] = placed(j, lambda i: own[k, i], moved[k, 0], moved[k, 1])
        spread_planes(mine.at[k], cells.at[k], k)

    def wide(ref_value):
        return ref_value.astype(F32).reshape(ch, plane)

    move(0)
    spread_planes(own.at[oldest], last, oldest)
    for k in range(1, oldest):
        move(k)
    for k in range(oldest):
        settle(k)

    r = lax.broadcasted_iota(jnp.int32, (plane, plane), 0)
    c = lax.broadcasted_iota(jnp.int32, (plane, plane), 1)
    ry, rz, cy, cz = r // side, r % side, c // side, c % side
    beside_cell = ((ry == cy) & (jnp.abs(rz - cz) == 1)) | ((rz == cz) & (jnp.abs(ry - cy) == 1))
    adj[...] = jnp.where(r == c, -6.0, jnp.where(beside_cell, 1.0, 0.0)).astype(BF16)
    width = 8 * side

    def layer_cell(layer, k):
        along_y = jnp.where(layer == 0, k, plane - side + k)
        along_z = jnp.where(layer == 2, k * side, k * side + side - 1)
        return jnp.where(layer < 2, along_y, along_z)

    r = lax.broadcasted_iota(jnp.int32, (plane, width), 0)
    c = lax.broadcasted_iota(jnp.int32, (plane, width), 1)
    for j in range(2):
        hit = (r == layer_cell((c // side) % 4, c % side)) & (c // (4 * side) == j)
        pick[j] = jnp.where(hit, 1.0, 0.0).astype(BF16)
    r = lax.broadcasted_iota(jnp.int32, (width, plane), 0)
    c = lax.broadcasted_iota(jnp.int32, (width, plane), 1)
    layer = (r // side) % 4
    opposite = jnp.where(layer % 2 == 0, layer + 1, layer - 1)
    place[...] = jnp.where(c == layer_cell(opposite, r % side), 1.0, 0.0).astype(BF16)
    bcol[...] = jnp.broadcast_to(bias[...], (bcol.shape[1], hid)).T
    loads[hist_len].wait()
    loads[hist_len + 1].wait()
    for k in range(hist_len + 1):
        wt[:, k * ch:(k + 1) * ch] = w_raw[k * ch:(k + 1) * ch, :].astype(F32).T.astype(BF16)
    wot[...] = wo_raw[...].astype(F32).T.astype(BF16)

    wait_for(last, go_recv.at[oldest])
    for to, which in enumerate((go_right, go_left)):
        stage_last[to] = jnp.where(which == 1, last[1], last[0])
    start_moves(stage_last, moved_last, oldest)

    lane = lax.broadcasted_iota(jnp.int32, (ch, width), 1)
    lane_layer, lane_patch = (lane // side) % 4, lane // (4 * side)

    def halo_copies(t, state, xm, xp, j):
        sem = lambda i: (halo_send.at[t, 5 * j + i], halo_recv.at[t, 5 * j + i])
        return (remote(state.at[j], xm.at[2 + j], *sem(0), (d, up)),
                remote(state.at[j], xp.at[2 + j], *sem(1), (d, down)))

    def rim_copies(t, state, buf, j):
        sem = lambda i: (halo_send.at[t, 5 * j + i], halo_recv.at[t, 5 * j + i])
        return ((has_right, remote(state.at[j], buf.at[j], *sem(2), (right, 1 - g))),
                (has_left, remote(state.at[j], buf.at[4 + j], *sem(3), (left, 1 - g))))

    def edge_copies(t, edge):
        return ((has_right, remote(edge.at[1], edge.at[0], halo_send.at[t, 4], halo_recv.at[t, 4], (right, g))),
                (has_left, remote(edge.at[1], edge.at[2], halo_send.at[t, 9], halo_recv.at[t, 9], (left, g))))

    def start_halo(t, state, xm, xp, j):
        for at, buf in ((0, xm), (1, xp)):
            for there, copy in rim_copies(t, state, buf, j):
                pl.when((g == at) & there)(copy.start)
        for copy in halo_copies(t, state, xm, xp, j):
            copy.start()

    def start_edges(t, state, edge):
        edges = sum(jnp.dot(wide(state[j]).astype(BF16), pick[j], preferred_element_type=F32) for j in range(2))
        edge[1] = edges.astype(BF16)
        for there, copy in edge_copies(t, edge):
            pl.when(there)(copy.start)

    def finish_halo(t, state, xm, xp, edge):
        for j in range(2):
            for copy in halo_copies(t, state, xm, xp, j):
                copy.wait()
            for at, out_buf, in_buf in ((0, xm, xp), (1, xp, xm)):
                (_, to_right), (_, to_left) = rim_copies(t, state, out_buf, j)
                (_, from_left), (_, from_right) = rim_copies(t, state, in_buf, j)
                for there, copy in ((has_right, to_right), (has_left, to_left)):
                    pl.when((g == at) & there)(copy.wait_send)
                for there, copy in ((has_left, from_left), (has_right, from_right)):
                    pl.when((g == at) & there)(copy.wait_recv)
        (_, right_edge), (_, left_edge) = edge_copies(t, edge)
        pl.when(has_right)(right_edge.wait_send)
        pl.when(has_left)(left_edge.wait_send)
        pl.when(has_left)(right_edge.wait_recv)
        pl.when(has_right)(left_edge.wait_recv)

    def laplace(state, xm, xp, edge, j):
        near = jnp.dot(wide(state[j]).astype(BF16), adj[...], preferred_element_type=F32)
        slots = beside_slot[j]
        wanted = jnp.where(lane_layer == 0, slots[3], jnp.where(lane_layer == 1, slots[2], jnp.where(
            lane_layer == 2, slots[5], slots[4])))
        faces = jnp.zeros((ch, width), F32)
        for i in range(3):
            faces = jnp.where(wanted == 2 * i + lane_patch, edge[i].astype(F32), faces)
        near = near + jnp.dot(faces.astype(BF16), place[...], preferred_element_type=F32)
        before = xm[jnp.where(my_plane == 0, slots[0], 2 + j)]
        after = xp[jnp.where(my_plane == grps - 1, slots[1], 2 + j)]
        return (near + wide(before) + wide(after)).astype(BF16)

    def times(k, rows):
        return jnp.dot(wt[:, k * ch:(k + 1) * ch], rows, preferred_element_type=F32)

    cols = [slice(j * plane, (j + 1) * plane) for j in range(2)]

    def next_state(pre, start, j):
        hidden = (pre / (1.0 + jnp.exp(-pre))).astype(BF16)
        update = jnp.dot(wot[...], hidden, preferred_element_type=F32).astype(BF16)
        fresh = start + step_size[j] * update.astype(F32)
        return fresh.reshape(grps, block, plane).astype(BF16)

    def send_back(t, state):
        def send(i, carry):
            peer = far_first(i)
            remote(state.at[:, peer], out.at[:, t, :, lanes_of(g)], back_send.at[t], back_recv.at[t],
                   (d, peer)).start()
            return carry

        lax.fori_loop(1, grps, send, 0)
        pltpu.make_async_copy(state.at[:, g], out.at[:, t, :, lanes_of(g)], back_recv.at[t]).start()

    newest = cells.at[0]
    wait_for(newest, go_recv.at[0])
    for j in range(2):
        start_halo(0, newest, xm1, xp1, j)
    start_edges(0, newest, edge1)
    wide_bias = jnp.concatenate([bcol[...]] * (plane // bcol.shape[1]), 1)
    for j in range(2):
        rows = wide(newest[j]).astype(BF16)
        base1[:, cols[j]] = wide_bias + times(0, rows)
        base2[:, cols[j]] = wide_bias + times(1, rows)
    arrived(stage_last, moved_last, oldest)
    for j in range(2):
        rows = placed(j, lambda i: last[i].astype(F32), moved_last[0].astype(F32), moved_last[1].astype(F32))
        base1[:, cols[j]] += times(oldest, rows.reshape(ch, plane).astype(BF16))
    finish_halo(0, newest, xm1, xp1, edge1)
    for j in range(2):
        base1[:, cols[j]] += times(hist_len, laplace(newest, xm1, xp1, edge1, j))
    for k in range(1, oldest - 1):
        wait_for(cells.at[k], go_recv.at[k])
        for j in range(2):
            rows = wide(cells[k, j]).astype(BF16)
            base1[:, cols[j]] += times(k, rows)
            base2[:, cols[j]] += times(k + 1, rows)
    wait_for(cells.at[oldest - 1], go_recv.at[oldest - 1])
    for j in range(2):
        pre = base1[:, cols[j]] + times(oldest - 1, wide(cells[oldest - 1, j]).astype(BF16))
        state1[j] = next_state(pre, wide(newest[j]), j)
        start_halo(1, state1, xm2, xp2, j)
    start_edges(1, state1, edge2)
    send_back(0, state1)
    for j in range(2):
        more = times(oldest, wide(cells[oldest - 1, j]).astype(BF16)) + times(0, wide(state1[j]).astype(BF16))
        base2[:, cols[j]] += more
    finish_halo(1, state1, xm2, xp2, edge2)
    for j in range(2):
        pre = base2[:, cols[j]] + times(hist_len, laplace(state1, xm2, xp2, edge2, j))
        state2[j] = next_state(pre, wide(state1[j]), j)
    send_back(1, state2)

    for k in range(hist_len):
        src, dst = (stage_last, moved_last) if k == oldest else (stage.at[k], moved.at[k])
        for there, copy in sent(src, dst, k):
            pl.when(there)(copy.wait_send)
        wait_for(last.at[:, pl.ds(0, grps - 1)], go_send.at[k])
    for t in range(2):
        wait_for(state1.at[:, pl.ds(0, grps - 1)], back_send.at[t])
        wait_for(out.at[:, t], back_recv.at[t])


def solution(mesh):
    doms, grps = mesh.shape["dom"], mesh.shape["grp"]

    def local(history, face_patch, refined, dest_slot, w_in, in_bias, w_out):
        per_dev, hist_len, block, cell_count = history.shape
        hid, ch = w_out.shape
        side = round(cell_count ** (1 / 3))
        plane = side * side
        width = 8 * side
        sizes = (doms, grps, side, hist_len, ch, hid)
        smem = pl.BlockSpec(memory_space=pltpu.SMEM)
        anywhere = pl.BlockSpec(memory_space=pl.ANY)
        vmem, dma = pltpu.VMEM, pltpu.SemaphoreType.DMA
        column = min(128, plane)
        states = pl.pallas_call(
            functools.partial(surrogate, sizes),
            out_shape=pltpu.VMEM((per_dev, 2, block, cell_count), BF16),
            in_specs=[smem, smem, smem, anywhere, anywhere, anywhere, pl.BlockSpec(memory_space=pltpu.VMEM)],
            out_specs=pl.BlockSpec(memory_space=pltpu.VMEM),
            scratch_shapes=[
                vmem((hist_len, per_dev, block, cell_count), BF16),
                *[vmem((hist_len - 1, 2, block, cell_count), BF16) for _ in range(3)],
                vmem((hist_len - 1, per_dev, grps, block, plane), BF16),
                *[vmem((2, grps, block, plane), BF16) for _ in range(3)],
                vmem((per_dev, grps, block, plane), BF16),
                vmem((per_dev, grps, block, plane), BF16),
                *[vmem((7, grps, block, plane), BF16) for _ in range(4)],
                *[vmem((3, ch, width), BF16) for _ in range(2)],
                vmem(w_in.shape, BF16),
                vmem(w_out.shape, BF16),
                vmem((hid, w_in.shape[0]), BF16),
                vmem((ch, hid), BF16),
                vmem((hid, column), F32),
                *[vmem((hid, per_dev * plane), F32) for _ in range(2)],
                vmem((plane, plane), BF16),
                vmem((2, plane, width), BF16),
                vmem((width, plane), BF16),
                dma((hist_len + 2,)),
                dma((hist_len, 2)),
                dma((hist_len, 2)),
                dma((hist_len,)),
                dma((hist_len,)),
                dma((2,)),
                dma((2,)),
                dma((2, 10)),
                dma((2, 10)),
            ],
            compiler_params=pltpu.CompilerParams(
                collective_id=0, has_side_effects=True, vmem_limit_bytes=60 * 2**20),
            name="surrogate",
        )(dest_slot, face_patch.T, refined, history, w_in, w_out, in_bias.reshape(1, hid))
        return states

    placed = (P("dom", None, "grp", None), P(), P(), P(), P(), P(), P())
    return jax.shard_map(
        local, mesh=mesh, in_specs=placed, out_specs=P("dom", None, "grp", None), check_vma=False
    )
```

time: 58.3 us -> 49.8 us (0.85)
  the two profiles are of different devices: /device:TPU:1 before, /device:TPU:113 now
where the time goes in v2:
time: 49.8 us; the launch traced here: 49.3 us
  Pallas kernels  48.6 us (98%)
  local copies, waits for them, and re-layouts  0.71 us (1%)
    pallas_call x1, Pallas kernels, local(): pl.pallas_call(functools.partial(surrogate, sizes), out_shape=pltpu.VMEM(...  48.6 us

profile of v2, /device:TPU:113, one launch (start us, length us, event | category | flops | bytes accessed | tf_op | source)
XLA Modules:
  0.0 49.3 jit_solution(12814658887260309633)
XLA Ops:
  0.0 48.6 %surrogate.1 = bf16[2,2,8,4096]{3,2,1,0:T(8,128)(2,1)S(1)} custom-call(s32[128]{0:T(128)} %dest.1, s32[6,128]{1,0:T(8,128)} %bitcast.2, s32[128]{0:T(128)} %refined.1, bf16[2,4,8,4096]{3,2,1,0:T(8,128)(2,1)} %hist.1, bf16[640,512]{1,0:T(8,128)(2,1)} %w_in.1, bf16[512,128]{1,0:T(8,128)(2,1)} %w_out.1, f32[1,512]{1,0:T(1,128)} %bitcast.3), custom_call_target="tpu_custom_call" | custom-call | tf_op jit(solution)/shard_map/surrogate/pallas_call | solution.py:321
  48.6 0.7 %copy.9 = bf16[2,2,8,4096]{3,2,1,0:T(8,128)(2,1)} copy(bf16[2,2,8,4096]{3,2,1,0:T(8,128)(2,1)S(1)} %surrogate.1) | data formatting | bytes 524288

commit v3 on v2

--- a/solution.py
+++ b/solution.py
@@ -11,14 +11,14 @@
 F32, BF16 = jnp.float32, jnp.bfloat16
 
 
-def surrogate(sizes, dest, face, refined, hist, w_in, w_out, bias, out, own, stage, moved, mine, cells, last, stage_last,
+def surrogate(sizes, dest_in, face_in, refined_in, hist, w_in, w_out, bias_in, out, dest, face, refined, bias, own, stage, moved, mine, cells, last, stage_last,
               moved_last, state1, state2, xm1, xp1, xm2, xp2, edge1, edge2, w_raw, wo_raw, wt, wot, bcol, base1, base2,
               adj, pick, place, load_sem, mig_send, mig_recv, go_send, go_recv, back_send, back_recv, halo_send,
               halo_recv):
     doms, grps, side, hist_len, ch, hid = sizes
     plane = side * side
     block = ch // grps
-    oldest = hist_len - 1
+    late = hist_len - 2
     d, g = lax.axis_index("dom"), lax.axis_index("grp")
     left, right = d - 1, d + 1
     has_left, has_right = d > 0, d < doms - 1
@@ -35,11 +35,17 @@
     loads = [pltpu.make_async_copy(hist.at[:, k], own.at[k], load_sem.at[k]) for k in range(hist_len)]
     loads.append(pltpu.make_async_copy(w_in, w_raw, load_sem.at[hist_len]))
     loads.append(pltpu.make_async_copy(w_out, wo_raw, load_sem.at[hist_len + 1]))
+    small = ((dest_in, dest), (face_in, face), (refined_in, refined), (bias_in, bias))
+    tables = [pltpu.make_async_copy(src, dst, load_sem.at[hist_len + 2 + i]) for i, (src, dst) in enumerate(small)]
+
+    def far_first(i):
+        half = lax.div(i, 2)
+        return lax.rem(g + grps // 2 + jnp.where(lax.rem(i, 2) == 0, half, -half), grps)
 
     barrier = pltpu.get_barrier_semaphore()
 
     def greet(i, carry):
-        pl.semaphore_signal(barrier, inc=1, device_id=(d, lax.rem(g + i, grps)), device_id_type=MESH)
+        pl.semaphore_signal(barrier, inc=1, device_id=(d, far_first(i)), device_id_type=MESH)
         return carry
 
     lax.fori_loop(1, grps, greet, 0)
@@ -52,8 +58,10 @@
             def _():
                 pl.semaphore_signal(barrier, inc=1, device_id=(beside, 1 - g), device_id_type=MESH)
 
-    for load in loads:
+    for load in tables + loads:
         load.start()
+    for table in tables:
+        table.wait()
 
     patches = 2 * doms
     cands = [lax.rem(2 * d + patches - 2 + i, patches) for i in range(6)]
@@ -111,10 +119,6 @@
     def lanes_of(device):
         return pl.ds(pl.multiple_of(lax.rem(device + grps - 1, grps) * plane, plane), plane)
 
-    def far_first(i):
-        half = lax.div(i, 2)
-        return lax.rem(g + grps // 2 + jnp.where(lax.rem(i, 2) == 0, half, -half), grps)
-
     def spread_planes(src, dst, k):
         def send(i, carry):
             peer = far_first(i)
@@ -134,10 +138,11 @@
         return ref_value.astype(F32).reshape(ch, plane)
 
     move(0)
-    spread_planes(own.at[oldest], last, oldest)
-    for k in range(1, oldest):
+    spread_planes(own.at[hist_len - 1], last.at[1], hist_len - 1)
+    for k in range(1, late):
         move(k)
-    for k in range(oldest):
+    spread_planes(own.at[late], last.at[0], late)
+    for k in range(late):
         settle(k)
 
     r = lax.broadcasted_iota(jnp.int32, (plane, plane), 0)
@@ -163,16 +168,17 @@
     opposite = jnp.where(layer % 2 == 0, layer + 1, layer - 1)
     place[...] = jnp.where(c == layer_cell(opposite, r % side), 1.0, 0.0).astype(BF16)
     bcol[...] = jnp.broadcast_to(bias[...], (bcol.shape[1], hid)).T
+    for k in (hist_len - 1, late):
+        r = k - late
+        wait_for(last.at[r], go_recv.at[k])
+        for to, which in enumerate((go_right, go_left)):
+            stage_last[r, to] = jnp.where(which == 1, last[r, 1], last[r, 0])
+        start_moves(stage_last.at[r], moved_last.at[r], k)
     loads[hist_len].wait()
     loads[hist_len + 1].wait()
     for k in range(hist_len + 1):
         wt[:, k * ch:(k + 1) * ch] = w_raw[k * ch:(k + 1) * ch, :].astype(F32).T.astype(BF16)
     wot[...] = wo_raw[...].astype(F32).T.astype(BF16)
-
-    wait_for(last, go_recv.at[oldest])
-    for to, which in enumerate((go_right, go_left)):
-        stage_last[to] = jnp.where(which == 1, last[1], last[0])
-    start_moves(stage_last, moved_last, oldest)
 
     lane = lax.broadcasted_iota(jnp.int32, (ch, width), 1)
     lane_layer, lane_patch = (lane // side) % 4, lane // (4 * side)
@@ -265,28 +271,32 @@
         rows = wide(newest[j]).astype(BF16)
         base1[:, cols[j]] = wide_bias + times(0, rows)
         base2[:, cols[j]] = wide_bias + times(1, rows)
-    arrived(stage_last, moved_last, oldest)
-    for j in range(2):
-        rows = placed(j, lambda i: last[i].astype(F32), moved_last[0].astype(F32), moved_last[1].astype(F32))
-        base1[:, cols[j]] += times(oldest, rows.reshape(ch, plane).astype(BF16))
+    for k in (hist_len - 1, late):
+        r = k - late
+        arrived(stage_last.at[r], moved_last.at[r], k)
+        for j in range(2):
+            rows = placed(j, lambda i: last[r, i].astype(F32), moved_last[r, 0].astype(F32), moved_last[r, 1].astype(F32))
+            rows = rows.reshape(ch, plane).astype(BF16)
+            base1[:, cols[j]] += times(k, rows)
+            if k + 1 < hist_len:
+                base2[:, cols[j]] += times(k + 1, rows)
     finish_halo(0, newest, xm1, xp1, edge1)
     for j in range(2):
         base1[:, cols[j]] += times(hist_len, laplace(newest, xm1, xp1, edge1, j))
-    for k in range(1, oldest - 1):
+    for k in range(1, late):
         wait_for(cells.at[k], go_recv.at[k])
-        for j in range(2):
-            rows = wide(cells[k, j]).astype(BF16)
-            base1[:, cols[j]] += times(k, rows)
-            base2[:, cols[j]] += times(k + 1, rows)
-    wait_for(cells.at[oldest - 1], go_recv.at[oldest - 1])
-    for j in range(2):
-        pre = base1[:, cols[j]] + times(oldest - 1, wide(cells[oldest - 1, j]).astype(BF16))
+    for j in range(2):
+        pre = base1[:, cols[j]]
+        for k in range(1, late):
+            pre = pre + times(k, wide(cells[k, j]).astype(BF16))
         state1[j] = next_state(pre, wide(newest[j]), j)
         start_halo(1, state1, xm2, xp2, j)
     start_edges(1, state1, edge2)
     send_back(0, state1)
     for j in range(2):
-        more = times(oldest, wide(cells[oldest - 1, j]).astype(BF16)) + times(0, wide(state1[j]).astype(BF16))
+        more = times(0, wide(state1[j]).astype(BF16))
+        for k in range(1, late):
+            more = more + times(k + 1, wide(cells[k, j]).astype(BF16))
         base2[:, cols[j]] += more
     finish_halo(1, state1, xm2, xp2, edge2)
     for j in range(2):
@@ -295,10 +305,10 @@
     send_back(1, state2)
 
     for k in range(hist_len):
-        src, dst = (stage_last, moved_last) if k == oldest else (stage.at[k], moved.at[k])
+        src, dst = (stage.at[k], moved.at[k]) if k < late else (stage_last.at[k - late], moved_last.at[k - late])
         for there, copy in sent(src, dst, k):
             pl.when(there)(copy.wait_send)
-        wait_for(last.at[:, pl.ds(0, grps - 1)], go_send.at[k])
+        wait_for(last.at[0, :, pl.ds(0, grps - 1)], go_send.at[k])
     for t in range(2):
         wait_for(state1.at[:, pl.ds(0, grps - 1)], back_send.at[t])
         wait_for(out.at[:, t], back_recv.at[t])
@@ -314,20 +324,23 @@
         plane = side * side
         width = 8 * side
         sizes = (doms, grps, side, hist_len, ch, hid)
-        smem = pl.BlockSpec(memory_space=pltpu.SMEM)
         anywhere = pl.BlockSpec(memory_space=pl.ANY)
         vmem, dma = pltpu.VMEM, pltpu.SemaphoreType.DMA
         column = min(128, plane)
         states = pl.pallas_call(
             functools.partial(surrogate, sizes),
             out_shape=pltpu.VMEM((per_dev, 2, block, cell_count), BF16),
-            in_specs=[smem, smem, smem, anywhere, anywhere, anywhere, pl.BlockSpec(memory_space=pltpu.VMEM)],
+            in_specs=[anywhere] * 7,
             out_specs=pl.BlockSpec(memory_space=pltpu.VMEM),
             scratch_shapes=[
+                pltpu.SMEM(dest_slot.shape, jnp.int32),
+                pltpu.SMEM(face_patch.shape[::-1], jnp.int32),
+                pltpu.SMEM(refined.shape, jnp.int32),
+                vmem((1, hid), F32),
                 vmem((hist_len, per_dev, block, cell_count), BF16),
-                *[vmem((hist_len - 1, 2, block, cell_count), BF16) for _ in range(3)],
-                vmem((hist_len - 1, per_dev, grps, block, plane), BF16),
-                *[vmem((2, grps, block, plane), BF16) for _ in range(3)],
+                *[vmem((hist_len - 2, 2, block, cell_count), BF16) for _ in range(3)],
+                vmem((hist_len - 2, per_dev, grps, block, plane), BF16),
+                *[vmem((2, 2, grps, block, plane), BF16) for _ in range(3)],
                 vmem((per_dev, grps, block, plane), BF16),
                 vmem((per_dev, grps, block, plane), BF16),
                 *[vmem((7, grps, block, plane), BF16) for _ in range(4)],
@@ -341,7 +354,7 @@
                 vmem((plane, plane), BF16),
                 vmem((2, plane, width), BF16),
                 vmem((width, plane), BF16),
-                dma((hist_len + 2,)),
+                dma((hist_len + 6,)),
                 dma((hist_len, 2)),
                 dma((hist_len, 2)),
                 dma((hist_len,)),

time: 49.8 us -> 49.1 us (0.986)
  no operation moved by 1% of the time
where the time goes in v3:
time: 49.1 us; the launch traced here: 48.9 us
  Pallas kernels  48.2 us (98%)
  local copies, waits for them, and re-layouts  0.71 us (1%)
    pallas_call x1, Pallas kernels, local(): pl.pallas_call(functools.partial(surrogate, sizes), out_shape=pltpu.VMEM(...  48.2 us

profile of v3, /device:TPU:113, one launch (start us, length us, event | category | flops | bytes accessed | tf_op | source)
XLA Modules:
  0.0 48.9 jit_solution(5793289041202801626)
XLA Ops:
  0.0 48.2 %surrogate.1 = bf16[2,2,8,4096]{3,2,1,0:T(8,128)(2,1)S(1)} custom-call(s32[128]{0:T(128)} %dest_in.1, s32[6,128]{1,0:T(8,128)} %bitcast.2, s32[128]{0:T(128)} %refined_in.1, bf16[2,4,8,4096]{3,2,1,0:T(8,128)(2,1)} %hist.1, bf16[640,512]{1,0:T(8,128)(2,1)} %w_in.1, bf16[512,128]{1,0:T(8,128)(2,1)} %w_out.1, f32[1,512]{1,0:T(1,128)} %bitcast.3), custom_call_target="tpu_custom_call" | custom-call | tf_op jit(solution)/shard_map/surrogate/pallas_call | solution.py:330
  48.2 0.7 %copy.9 = bf16[2,2,8,4096]{3,2,1,0:T(8,128)(2,1)} copy(bf16[2,2,8,4096]{3,2,1,0:T(8,128)(2,1)S(1)} %surrogate.1) | data formatting | bytes 524288

commit v4 on v3

--- a/solution.py
+++ b/solution.py
@@ -42,6 +42,10 @@
         half = lax.div(i, 2)
         return lax.rem(g + grps // 2 + jnp.where(lax.rem(i, 2) == 0, half, -half), grps)
 
+    first = [loads[0]] + loads[late:hist_len]
+    for load in first:
+        load.start()
+
     barrier = pltpu.get_barrier_semaphore()
 
     def greet(i, carry):
@@ -58,7 +62,7 @@
             def _():
                 pl.semaphore_signal(barrier, inc=1, device_id=(beside, 1 - g), device_id_type=MESH)
 
-    for load in tables + loads:
+    for load in tables + loads[1:late] + loads[hist_len:]:
         load.start()
     for table in tables:
         table.wait()
@@ -93,8 +97,8 @@
 
     for buf in (xm1, xp1, xm2, xp2):
         buf[6] = jnp.zeros(buf.shape[1:], BF16)
-    for k in range(hist_len):
-        loads[k].wait()
+    for load in first:
+        load.wait()
     beside_count = jnp.where(has_left, 1, 0) + jnp.where(has_right, 1, 0)
     pl.semaphore_wait(barrier, grps - 1 + beside_count * jnp.where(g < 2, 2, 1))
 
@@ -138,10 +142,18 @@
         return ref_value.astype(F32).reshape(ch, plane)
 
     move(0)
-    spread_planes(own.at[hist_len - 1], last.at[1], hist_len - 1)
+
+    def send_late(i, carry):
+        peer = far_first(i)
+        remote(own.at[pl.ds(late, 2), :, :, lanes_of(peer)], last.at[:, :, g], go_send.at[late], go_recv.at[late],
+               (d, peer)).start()
+        return carry
+
+    lax.fori_loop(1, grps, send_late, 0)
+    pltpu.make_async_copy(own.at[pl.ds(late, 2), :, :, lanes_of(g)], last.at[:, :, g], go_recv.at[late]).start()
     for k in range(1, late):
+        loads[k].wait()
         move(k)
-    spread_planes(own.at[late], last.at[0], late)
     for k in range(late):
         settle(k)
 
@@ -168,9 +180,9 @@
     opposite = jnp.where(layer % 2 == 0, layer + 1, layer - 1)
     place[...] = jnp.where(c == layer_cell(opposite, r % side), 1.0, 0.0).astype(BF16)
     bcol[...] = jnp.broadcast_to(bias[...], (bcol.shape[1], hid)).T
+    wait_for(last, go_recv.at[late])
     for k in (hist_len - 1, late):
         r = k - late
-        wait_for(last.at[r], go_recv.at[k])
         for to, which in enumerate((go_right, go_left)):
             stage_last[r, to] = jnp.where(which == 1, last[r, 1], last[r, 0])
         start_moves(stage_last.at[r], moved_last.at[r], k)
@@ -308,7 +320,9 @@
         src, dst = (stage.at[k], moved.at[k]) if k < late else (stage_last.at[k - late], moved_last.at[k - late])
         for there, copy in sent(src, dst, k):
             pl.when(there)(copy.wait_send)
-        wait_for(last.at[0, :, pl.ds(0, grps - 1)], go_send.at[k])
+        if k < late:
+            wait_for(last.at[0, :, pl.ds(0, grps - 1)], go_send.at[k])
+    wait_for(last.at[:, :, pl.ds(0, grps - 1)], go_send.at[late])
     for t in range(2):
         wait_for(state1.at[:, pl.ds(0, grps - 1)], back_send.at[t])
         wait_for(out.at[:, t], back_recv.at[t])

time: 49.1 us -> 48.9 us (level)
  no operation moved by 1% of the time
where the time goes in v4:
time: 48.9 us; the launch traced here: 48.8 us
  Pallas kernels  48 us (98%)
  local copies, waits for them, and re-layouts  0.71 us (1%)
    pallas_call x1, Pallas kernels, local(): pl.pallas_call(functools.partial(surrogate, sizes), out_shape=pltpu.VMEM(...  48 us

profile of v4, /device:TPU:113, one launch (start us, length us, event | category | flops | bytes accessed | tf_op | source)
XLA Modules:
  0.0 48.8 jit_solution(10040601160010005376)
XLA Ops:
  0.0 48.0 %surrogate.1 = bf16[2,2,8,4096]{3,2,1,0:T(8,128)(2,1)S(1)} custom-call(s32[128]{0:T(128)} %dest_in.1, s32[6,128]{1,0:T(8,128)} %bitcast.2, s32[128]{0:T(128)} %refined_in.1, bf16[2,4,8,4096]{3,2,1,0:T(8,128)(2,1)} %hist.1, bf16[640,512]{1,0:T(8,128)(2,1)} %w_in.1, bf16[512,128]{1,0:T(8,128)(2,1)} %w_out.1, f32[1,512]{1,0:T(1,128)} %bitcast.3), custom_call_target="tpu_custom_call" | custom-call | tf_op jit(solution)/shard_map/surrogate/pallas_call | solution.py:344
  48.1 0.7 %copy.9 = bf16[2,2,8,4096]{3,2,1,0:T(8,128)(2,1)} copy(bf16[2,2,8,4096]{3,2,1,0:T(8,128)(2,1)S(1)} %surrogate.1) | data formatting | bytes 524288

commit v5 on v4

--- a/solution.py
+++ b/solution.py
@@ -141,8 +141,6 @@
     def wide(ref_value):
         return ref_value.astype(F32).reshape(ch, plane)
 
-    move(0)
-
     def send_late(i, carry):
         peer = far_first(i)
         remote(own.at[pl.ds(late, 2), :, :, lanes_of(peer)], last.at[:, :, g], go_send.at[late], go_recv.at[late],
@@ -151,6 +149,7 @@
 
     lax.fori_loop(1, grps, send_late, 0)
     pltpu.make_async_copy(own.at[pl.ds(late, 2), :, :, lanes_of(g)], last.at[:, :, g], go_recv.at[late]).start()
+    move(0)
     for k in range(1, late):
         loads[k].wait()
         move(k)

time: 48.9 us -> 49.1 us (level)
  no operation moved by 1% of the time
where the time goes in v5:
time: 49.1 us; the launch traced here: 49 us
  Pallas kernels  48.3 us (98%)
  local copies, waits for them, and re-layouts  0.71 us (1%)
    pallas_call x1, Pallas kernels, local(): pl.pallas_call(functools.partial(surrogate, sizes), out_shape=pltpu.VMEM(...  48.3 us

profile of v5, /device:TPU:113, one launch (start us, length us, event | category | flops | bytes accessed | tf_op | source)
XLA Modules:
  0.0 49.0 jit_solution(11468127003848567844)
XLA Ops:
  0.0 48.3 %surrogate.1 = bf16[2,2,8,4096]{3,2,1,0:T(8,128)(2,1)S(1)} custom-call(s32[128]{0:T(128)} %dest_in.1, s32[6,128]{1,0:T(8,128)} %bitcast.2, s32[128]{0:T(128)} %refined_in.1, bf16[2,4,8,4096]{3,2,1,0:T(8,128)(2,1)} %hist.1, bf16[640,512]{1,0:T(8,128)(2,1)} %w_in.1, bf16[512,128]{1,0:T(8,128)(2,1)} %w_out.1, f32[1,512]{1,0:T(1,128)} %bitcast.3), custom_call_target="tpu_custom_call" | custom-call | tf_op jit(solution)/shard_map/surrogate/pallas_call | solution.py:343
  48.3 0.7 %copy.9 = bf16[2,2,8,4096]{3,2,1,0:T(8,128)(2,1)} copy(bf16[2,2,8,4096]{3,2,1,0:T(8,128)(2,1)S(1)} %surrogate.1) | data formatting | bytes 524288
